TPU v7x, 32 devices: a whole 2x2x4 slice. The times are simulated.
32 devices in a mesh: dp: 4 (over x, core), fsdp: 8 (over z, y).
Axes of the slice: x: 2, y: 2, z: 4, core: 2. Of those that a mesh axis runs over, the one named last changes fastest.
Arguments:
- attention_input: bfloat16 [8192, 768], P('fsdp', 'dp')
- feedforward_input: bfloat16 [14336, 768], P('fsdp', 'dp')
- attention_cotangent: bfloat16 [8192, 768], P(('dp', 'fsdp'))
- feedforward_cotangent: bfloat16 [8192, 768], P(('dp', 'fsdp'))
- lengths: int32 [12], replicated, may hold values from 16 to 64, as said below
- groups: int32 [12], replicated, may hold values from 0 to 3, as said below
- attention_weight: bfloat16 [8192, 8192], P('fsdp', 'dp'), may hold values from -0.29882812 to 0.29882812
- attention_moment: bfloat16 [8192, 8192], P('fsdp', 'dp'), may hold values from -0.59765625 to 0.59765625
- attention_second: bfloat16 [8192, 8192], P('fsdp', 'dp'), may hold values from 0.0099487305 to 1
- feedforward_weight: bfloat16 [14336, 8192], P('fsdp', 'dp'), may hold values from -0.29882812 to 0.29882812
- feedforward_moment: bfloat16 [14336, 8192], P('fsdp', 'dp'), may hold values from -0.59765625 to 0.59765625
- feedforward_second: bfloat16 [14336, 8192], P('fsdp', 'dp'), may hold values from 0.0099487305 to 1
Outputs:
- new_attention_weight: bfloat16 [8192, 8192], P('fsdp', 'dp')
- new_attention_moment: bfloat16 [8192, 8192], P('fsdp', 'dp')
- new_attention_second: bfloat16 [8192, 8192], P('fsdp', 'dp')
- new_feedforward_weight: bfloat16 [14336, 8192], P('fsdp', 'dp')
- new_feedforward_moment: bfloat16 [14336, 8192], P('fsdp', 'dp')
- new_feedforward_second: bfloat16 [14336, 8192], P('fsdp', 'dp')
Inputs may be any that keep to these rules, and one draw needn't show every extreme that they name: `lengths`: some example has exactly 64 live tokens. `groups`: every group has at least one example.
All inputs are finite; a program needn't handle non-finite values.
Results may differ from a plain program's by a relative error of at most 0.0038.
Values may be sent and summed in bfloat16 or wider, within the bound.
A program may use at most 192 MiB of HBM per device.

v0:
```python
import jax
import jax.numpy as jnp
from jax import lax
from jax.sharding import PartitionSpec as P

first_decay = 0.9
second_decay = 0.95
first_bias = 1.0 - 0.9**10
second_bias = 1.0 - 0.95**10
learn_rate = 0.01
weight_decay = 0.1
epsilon = 1e-08
norm_epsilon = 1e-06


def live_tokens(lengths, slot_len):
    position = lax.broadcasted_iota(jnp.int32, (lengths.shape[0], slot_len), 1)
    return (position < lengths[:, None]).reshape(-1)


def example_norms(inputs, cotangents, second, slot_len):
    precond = 1.0 / (jnp.sqrt(second.astype(jnp.float32)) + epsilon)
    example_count = inputs.shape[1] // slot_len

    def one_example(example, norm_vals):
        inputs_slot = lax.dynamic_slice_in_dim(inputs, example * slot_len, slot_len, 1)
        grads_slot = lax.dynamic_slice_in_dim(cotangents, example * slot_len, slot_len, 1)
        tile_block = lax.dot_general(
            inputs_slot, grads_slot, (((1,), (1,)), ((), ())), preferred_element_type=jnp.float32
        )
        return norm_vals.at[example].set(jnp.sum(tile_block * tile_block * precond))

    return lax.fori_loop(0, example_count, one_example, jnp.zeros((example_count,), jnp.float32))


def importance(norm_vals, groups):
    strength = jnp.sqrt(norm_vals + norm_epsilon)
    same_group = (groups[:, None] == groups[None, :]).astype(jnp.float32)
    group_total = jnp.sum(same_group * strength[None, :], axis=1)
    group_count = jnp.sum(same_group, axis=1)
    return group_count * strength / group_total


def weighted_gradient(inputs, cotangents, token_weight, example_count):
    scaled = (inputs.astype(jnp.float32) * token_weight[None, :]).astype(jnp.bfloat16)
    product = lax.dot_general(
        scaled, cotangents, (((1,), (1,)), ((), ())), preferred_element_type=jnp.float32
    )
    return product / example_count


def adamw_step(weight, moment, second, gradient):
    moment_new = first_decay * moment.astype(jnp.float32) + (1.0 - first_decay) * gradient
    second_new = (
        second_decay * second.astype(jnp.float32) + (1.0 - second_decay) * gradient * gradient
    )
    step_dir = moment_new / first_bias / (jnp.sqrt(second_new / second_bias) + epsilon)
    weight_wide = weight.astype(jnp.float32)
    updated = weight_wide - learn_rate * (step_dir + weight_decay * weight_wide)
    return (
        updated.astype(jnp.bfloat16),
        moment_new.astype(jnp.bfloat16),
        second_new.astype(jnp.bfloat16),
    )


def per_device(
    attention_input,
    feedforward_input,
    attention_cotangent,
    feedforward_cotangent,
    lengths,
    groups,
    attention_weight,
    attention_moment,
    attention_second,
    feedforward_weight,
    feedforward_moment,
    feedforward_second,
):
    example_count = lengths.shape[0]
    attention_full, feedforward_full = (
        lax.all_gather(attention_input, "dp", axis=1, tiled=True),
        lax.all_gather(feedforward_input, "dp", axis=1, tiled=True),
    )
    slot_len = attention_full.shape[1] // example_count
    live_mask = live_tokens(lengths, slot_len)
    attention_live = jnp.where(live_mask[None, :], attention_full, jnp.zeros_like(attention_full))
    feedforward_live = jnp.where(
        live_mask[None, :], feedforward_full, jnp.zeros_like(feedforward_full)
    )
    attention_columns, feedforward_columns = (
        lax.all_gather(attention_cotangent, "fsdp", axis=0, tiled=True),
        lax.all_gather(feedforward_cotangent, "fsdp", axis=0, tiled=True),
    )
    attention_part = example_norms(attention_live, attention_columns, attention_second, slot_len)
    feedforward_part = example_norms(
        feedforward_live, feedforward_columns, feedforward_second, slot_len
    )
    norm_vals = lax.psum(attention_part + feedforward_part, ("dp", "fsdp"))
    weights = importance(norm_vals, groups)
    token_weight = jnp.repeat(weights, slot_len) * live_mask.astype(jnp.float32)
    attention_grad = weighted_gradient(
        attention_live, attention_columns, token_weight, example_count
    )
    feedforward_grad = weighted_gradient(
        feedforward_live, feedforward_columns, token_weight, example_count
    )
    attention_new = adamw_step(attention_weight, attention_moment, attention_second, attention_grad)
    feedforward_new = adamw_step(
        feedforward_weight, feedforward_moment, feedforward_second, feedforward_grad
    )
    return (
        attention_new[0],
        attention_new[1],
        attention_new[2],
        feedforward_new[0],
        feedforward_new[1],
        feedforward_new[2],
    )


def solution(mesh):
    return jax.shard_map(
        per_device,
        mesh=mesh,
        in_specs=(
            P("fsdp", "dp"),
            P("fsdp", "dp"),
            P(("dp", "fsdp"), None),
            P(("dp", "fsdp"), None),
            P(),
            P(),
            P("fsdp", "dp"),
            P("fsdp", "dp"),
            P("fsdp", "dp"),
            P("fsdp", "dp"),
            P("fsdp", "dp"),
            P("fsdp", "dp"),
        ),
        out_specs=(
            P("fsdp", "dp"),
            P("fsdp", "dp"),
            P("fsdp", "dp"),
            P("fsdp", "dp"),
            P("fsdp", "dp"),
            P("fsdp", "dp"),
        ),
        check_vma=False,
    )
```

profile of v0, /device:TPU:0, one launch (start us, length us, event | category | flops | bytes accessed | tf_op | source)
XLA Modules:
  0.0 432.2 jit_solution(12337286878783757687)
XLA Ops:
  7.2 0.7 all-gather.5.cloned.1.call-update
  7.9 0.7 all-gather.9.cloned.1.call-update
  8.7 0.7 all-gather.11.cloned.1.call-update
  10.0 0.7 iota_compare_fusion
  10.8 13.4 %fusion.7 = f32[1792,2048]{1,0:T(8,128)} fusion(bf16[1792,2048]{1,0:T(8,128)(2,1)} %param.31), kind=kLoop, calls=%fused_computation.15 | loop fusion | flops 11010048 | bytes 22020096 | tf_op jit(solution)/shard_map/div | solution.py:22
  24.2 6.0 %fusion.17 = f32[1024,2048]{1,0:T(8,128)} fusion(bf16[1024,2048]{1,0:T(8,128)(2,1)S(1)} %copy-done), kind=kLoop, calls=%fused_computation.30 | loop fusion | flops 6291456 | bytes 12582912 | tf_op jit(solution)/shard_map/div | solution.py:22
  30.2 1.8 all-gather.5.cloned.1.call-done
  31.9 2.7 broadcast_select_fusion.1
  34.7 25.2 %all-gather.9.cloned.1.call-done = bf16[1792,768]{0,1:T(8,128)(2,1)} async-done(((bf16[1792,192]{0,1:T(8,128)(2,1)}), bf16[1792,768]{0,1:T(8,128)(2,1)}) %all-gather.9.cloned.1.call-update) | async-done | bytes 2752528 | tf_op jit(solution)/shard_map/all_gather | solution.py:84
  59.8 2.0 broadcast_select_fusion
  61.9 60.6 %all-gather.11.cloned.1.call-done = bf16[2048,768]{1,0:T(8,128)(2,1)} async-done(((bf16[256,768]{1,0:T(8,128)(2,1)}), bf16[2048,768]{1,0:T(8,128)(2,1)}) %all-gather.11.cloned.1.call-update) | async-done | bytes 3145744 | tf_op jit(solution)/shard_map/all_gather | solution.py:94
  122.5 131.0 %while.29 = (s32[]{:T(128)}, f32[12]{0:T(128)S(1)}, bf16[1792,768]{0,1:T(8,128)(2,1)S(1)}, bf16[2048,768]{1,0:T(8,128)(2,1)}, f32[1792,2048]{1,0:T(8,128)}, /*in...) while((s32[]{:T(128)}, f32[12]{0:T(128)S(1)}, bf16[1792,768]{0,1:T(8,128)(2,1)S(1)}, ...), condition=%wide.region_6.7_spmd, body=%wide.region_4.6_spmd.sunk | while | flops 480772096 | bytes 15435029 | solution.py:33
  122.5 10.1 %multiply_reduce_fusion.5 = f32[]{:T(128)} fusion(f32[1792,2048]{1,0:T(8,128)} %get-tuple-element.404, bf16[2048,768]{1,0:T(8,128)(2,1)} %get-tuple-element.403, s32[]{:T(128)S(6)} %select_n.41, bf16[1792,768]{0,1:T(8,128)(2,1)S(1)} %get-tuple-element.402), kind=kOutput, calls=%fused_computation.5.clone.1 | convolution fusion | flops 480772096 | bytes 15434756 | tf_op jit(solution)/shard_map/while/body/eval_jaxpr/dot_general | solution.py:28
  132.6 0.8 select_dynamic-update-slice_fusion.5
  133.4 10.1 %multiply_reduce_fusion.5 = f32[]{:T(128)} fusion(f32[1792,2048]{1,0:T(8,128)} %get-tuple-element.404, bf16[2048,768]{1,0:T(8,128)(2,1)} %get-tuple-element.403, s32[]{:T(128)S(6)} %select_n.41, bf16[1792,768]{0,1:T(8,128)(2,1)S(1)} %get-tuple-element.402), kind=kOutput, calls=%fused_computation.5.clone.1 | convolution fusion | flops 480772096 | bytes 15434756 | tf_op jit(solution)/shard_map/while/body/eval_jaxpr/dot_general | solution.py:28
  143.6 0.8 select_dynamic-update-slice_fusion.5
  144.4 10.1 %multiply_reduce_fusion.5 = f32[]{:T(128)} fusion(f32[1792,2048]{1,0:T(8,128)} %get-tuple-element.404, bf16[2048,768]{1,0:T(8,128)(2,1)} %get-tuple-element.403, s32[]{:T(128)S(6)} %select_n.41, bf16[1792,768]{0,1:T(8,128)(2,1)S(1)} %get-tuple-element.402), kind=kOutput, calls=%fused_computation.5.clone.1 | convolution fusion | flops 480772096 | bytes 15434756 | tf_op jit(solution)/shard_map/while/body/eval_jaxpr/dot_general | solution.py:28
  154.5 0.8 select_dynamic-update-slice_fusion.5
  155.3 10.1 %multiply_reduce_fusion.5 = f32[]{:T(128)} fusion(f32[1792,2048]{1,0:T(8,128)} %get-tuple-element.404, bf16[2048,768]{1,0:T(8,128)(2,1)} %get-tuple-element.403, s32[]{:T(128)S(6)} %select_n.41, bf16[1792,768]{0,1:T(8,128)(2,1)S(1)} %get-tuple-element.402), kind=kOutput, calls=%fused_computation.5.clone.1 | convolution fusion | flops 480772096 | bytes 15434756 | tf_op jit(solution)/shard_map/while/body/eval_jaxpr/dot_general | solution.py:28
  165.4 0.8 select_dynamic-update-slice_fusion.5
  166.2 10.1 %multiply_reduce_fusion.5 = f32[]{:T(128)} fusion(f32[1792,2048]{1,0:T(8,128)} %get-tuple-element.404, bf16[2048,768]{1,0:T(8,128)(2,1)} %get-tuple-element.403, s32[]{:T(128)S(6)} %select_n.41, bf16[1792,768]{0,1:T(8,128)(2,1)S(1)} %get-tuple-element.402), kind=kOutput, calls=%fused_computation.5.clone.1 | convolution fusion | flops 480772096 | bytes 15434756 | tf_op jit(solution)/shard_map/while/body/eval_jaxpr/dot_general | solution.py:28
  176.3 0.8 select_dynamic-update-slice_fusion.5
  177.2 10.1 %multiply_reduce_fusion.5 = f32[]{:T(128)} fusion(f32[1792,2048]{1,0:T(8,128)} %get-tuple-element.404, bf16[2048,768]{1,0:T(8,128)(2,1)} %get-tuple-element.403, s32[]{:T(128)S(6)} %select_n.41, bf16[1792,768]{0,1:T(8,128)(2,1)S(1)} %get-tuple-element.402), kind=kOutput, calls=%fused_computation.5.clone.1 | convolution fusion | flops 480772096 | bytes 15434756 | tf_op jit(solution)/shard_map/while/body/eval_jaxpr/dot_general | solution.py:28
  187.2 0.8 select_dynamic-update-slice_fusion.5
  188.1 10.1 %multiply_reduce_fusion.5 = f32[]{:T(128)} fusion(f32[1792,2048]{1,0:T(8,128)} %get-tuple-element.404, bf16[2048,768]{1,0:T(8,128)(2,1)} %get-tuple-element.403, s32[]{:T(128)S(6)} %select_n.41, bf16[1792,768]{0,1:T(8,128)(2,1)S(1)} %get-tuple-element.402), kind=kOutput, calls=%fused_computation.5.clone.1 | convolution fusion | flops 480772096 | bytes 15434756 | tf_op jit(solution)/shard_map/while/body/eval_jaxpr/dot_general | solution.py:28
  198.2 0.8 select_dynamic-update-slice_fusion.5
  199.0 10.1 %multiply_reduce_fusion.5 = f32[]{:T(128)} fusion(f32[1792,2048]{1,0:T(8,128)} %get-tuple-element.404, bf16[2048,768]{1,0:T(8,128)(2,1)} %get-tuple-element.403, s32[]{:T(128)S(6)} %select_n.41, bf16[1792,768]{0,1:T(8,128)(2,1)S(1)} %get-tuple-element.402), kind=kOutput, calls=%fused_computation.5.clone.1 | convolution fusion | flops 480772096 | bytes 15434756 | tf_op jit(solution)/shard_map/while/body/eval_jaxpr/dot_general | solution.py:28
  209.1 0.8 select_dynamic-update-slice_fusion.5
  209.9 10.1 %multiply_reduce_fusion.5 = f32[]{:T(128)} fusion(f32[1792,2048]{1,0:T(8,128)} %get-tuple-element.404, bf16[2048,768]{1,0:T(8,128)(2,1)} %get-tuple-element.403, s32[]{:T(128)S(6)} %select_n.41, bf16[1792,768]{0,1:T(8,128)(2,1)S(1)} %get-tuple-element.402), kind=kOutput, calls=%fused_computation.5.clone.1 | convolution fusion | flops 480772096 | bytes 15434756 | tf_op jit(solution)/shard_map/while/body/eval_jaxpr/dot_general | solution.py:28
  220.0 0.8 select_dynamic-update-slice_fusion.5
  220.8 10.1 %multiply_reduce_fusion.5 = f32[]{:T(128)} fusion(f32[1792,2048]{1,0:T(8,128)} %get-tuple-element.404, bf16[2048,768]{1,0:T(8,128)(2,1)} %get-tuple-element.403, s32[]{:T(128)S(6)} %select_n.41, bf16[1792,768]{0,1:T(8,128)(2,1)S(1)} %get-tuple-element.402), kind=kOutput, calls=%fused_computation.5.clone.1 | convolution fusion | flops 480772096 | bytes 15434756 | tf_op jit(solution)/shard_map/while/body/eval_jaxpr/dot_general | solution.py:28
  230.9 0.8 select_dynamic-update-slice_fusion.5
  231.7 10.1 %multiply_reduce_fusion.5 = f32[]{:T(128)} fusion(f32[1792,2048]{1,0:T(8,128)} %get-tuple-element.404, bf16[2048,768]{1,0:T(8,128)(2,1)} %get-tuple-element.403, s32[]{:T(128)S(6)} %select_n.41, bf16[1792,768]{0,1:T(8,128)(2,1)S(1)} %get-tuple-element.402), kind=kOutput, calls=%fused_computation.5.clone.1 | convolution fusion | flops 480772096 | bytes 15434756 | tf_op jit(solution)/shard_map/while/body/eval_jaxpr/dot_general | solution.py:28
  241.8 0.8 select_dynamic-update-slice_fusion.5
  242.6 10.1 %multiply_reduce_fusion.5 = f32[]{:T(128)} fusion(f32[1792,2048]{1,0:T(8,128)} %get-tuple-element.404, bf16[2048,768]{1,0:T(8,128)(2,1)} %get-tuple-element.403, s32[]{:T(128)S(6)} %select_n.41, bf16[1792,768]{0,1:T(8,128)(2,1)S(1)} %get-tuple-element.402), kind=kOutput, calls=%fused_computation.5.clone.1 | convolution fusion | flops 480772096 | bytes 15434756 | tf_op jit(solution)/shard_map/while/body/eval_jaxpr/dot_general | solution.py:28
  252.7 0.8 select_dynamic-update-slice_fusion.5
  253.5 90.1 %while.28 = (s32[]{:T(128)}, f32[12]{0:T(128)S(1)}, bf16[1024,768]{0,1:T(8,128)(2,1)}, bf16[2048,768]{1,0:T(8,128)(2,1)}, f32[1024,2048]{1,0:T(8,128)}, /*index=...) while((s32[]{:T(128)}, f32[12]{0:T(128)S(1)}, bf16[1024,768]{0,1:T(8,128)(2,1)}, ...), condition=%wide.region_3.4_spmd, body=%wide.region_1.0_spmd.sunk | while | flops 274726912 | bytes 9045269 | solution.py:33
  253.5 6.7 %multiply_reduce_fusion.4 = f32[]{:T(128)} fusion(f32[1024,2048]{1,0:T(8,128)} %get-tuple-element.374, bf16[2048,768]{1,0:T(8,128)(2,1)} %get-tuple-element.373, s32[]{:T(128)S(6)} %select_n.40, bf16[1024,768]{0,1:T(8,128)(2,1)} %get-tuple-element.372), kind=kOutput, calls=%fused_computation.clone.1 | convolution fusion | flops 274726912 | bytes 9044996 | tf_op jit(solution)/shard_map/while/body/eval_jaxpr/dot_general | solution.py:28
  260.2 0.8 select_dynamic-update-slice_fusion.4
  261.0 6.7 %multiply_reduce_fusion.4 = f32[]{:T(128)} fusion(f32[1024,2048]{1,0:T(8,128)} %get-tuple-element.374, bf16[2048,768]{1,0:T(8,128)(2,1)} %get-tuple-element.373, s32[]{:T(128)S(6)} %select_n.40, bf16[1024,768]{0,1:T(8,128)(2,1)} %get-tuple-element.372), kind=kOutput, calls=%fused_computation.clone.1 | convolution fusion | flops 274726912 | bytes 9044996 | tf_op jit(solution)/shard_map/while/body/eval_jaxpr/dot_general | solution.py:28
  267.7 0.8 select_dynamic-update-slice_fusion.4
  268.5 6.7 %multiply_reduce_fusion.4 = f32[]{:T(128)} fusion(f32[1024,2048]{1,0:T(8,128)} %get-tuple-element.374, bf16[2048,768]{1,0:T(8,128)(2,1)} %get-tuple-element.373, s32[]{:T(128)S(6)} %select_n.40, bf16[1024,768]{0,1:T(8,128)(2,1)} %get-tuple-element.372), kind=kOutput, calls=%fused_computation.clone.1 | convolution fusion | flops 274726912 | bytes 9044996 | tf_op jit(solution)/shard_map/while/body/eval_jaxpr/dot_general | solution.py:28
  275.2 0.8 select_dynamic-update-slice_fusion.4
  276.0 6.7 %multiply_reduce_fusion.4 = f32[]{:T(128)} fusion(f32[1024,2048]{1,0:T(8,128)} %get-tuple-element.374, bf16[2048,768]{1,0:T(8,128)(2,1)} %get-tuple-element.373, s32[]{:T(128)S(6)} %select_n.40, bf16[1024,768]{0,1:T(8,128)(2,1)} %get-tuple-element.372), kind=kOutput, calls=%fused_computation.clone.1 | convolution fusion | flops 274726912 | bytes 9044996 | tf_op jit(solution)/shard_map/while/body/eval_jaxpr/dot_general | solution.py:28
  282.7 0.8 select_dynamic-update-slice_fusion.4
  283.5 6.7 %multiply_reduce_fusion.4 = f32[]{:T(128)} fusion(f32[1024,2048]{1,0:T(8,128)} %get-tuple-element.374, bf16[2048,768]{1,0:T(8,128)(2,1)} %get-tuple-element.373, s32[]{:T(128)S(6)} %select_n.40, bf16[1024,768]{0,1:T(8,128)(2,1)} %get-tuple-element.372), kind=kOutput, calls=%fused_computation.clone.1 | convolution fusion | flops 274726912 | bytes 9044996 | tf_op jit(solution)/shard_map/while/body/eval_jaxpr/dot_general | solution.py:28
  290.2 0.8 select_dynamic-update-slice_fusion.4
  291.0 6.7 %multiply_reduce_fusion.4 = f32[]{:T(128)} fusion(f32[1024,2048]{1,0:T(8,128)} %get-tuple-element.374, bf16[2048,768]{1,0:T(8,128)(2,1)} %get-tuple-element.373, s32[]{:T(128)S(6)} %select_n.40, bf16[1024,768]{0,1:T(8,128)(2,1)} %get-tuple-element.372), kind=kOutput, calls=%fused_computation.clone.1 | convolution fusion | flops 274726912 | bytes 9044996 | tf_op jit(solution)/shard_map/while/body/eval_jaxpr/dot_general | solution.py:28
  297.7 0.8 select_dynamic-update-slice_fusion.4
  298.6 6.7 %multiply_reduce_fusion.4 = f32[]{:T(128)} fusion(f32[1024,2048]{1,0:T(8,128)} %get-tuple-element.374, bf16[2048,768]{1,0:T(8,128)(2,1)} %get-tuple-element.373, s32[]{:T(128)S(6)} %select_n.40, bf16[1024,768]{0,1:T(8,128)(2,1)} %get-tuple-element.372), kind=kOutput, calls=%fused_computation.clone.1 | convolution fusion | flops 274726912 | bytes 9044996 | tf_op jit(solution)/shard_map/while/body/eval_jaxpr/dot_general | solution.py:28
  305.2 0.8 select_dynamic-update-slice_fusion.4
  306.1 6.7 %multiply_reduce_fusion.4 = f32[]{:T(128)} fusion(f32[1024,2048]{1,0:T(8,128)} %get-tuple-element.374, bf16[2048,768]{1,0:T(8,128)(2,1)} %get-tuple-element.373, s32[]{:T(128)S(6)} %select_n.40, bf16[1024,768]{0,1:T(8,128)(2,1)} %get-tuple-element.372), kind=kOutput, calls=%fused_computation.clone.1 | convolution fusion | flops 274726912 | bytes 9044996 | tf_op jit(solution)/shard_map/while/body/eval_jaxpr/dot_general | solution.py:28
  312.8 0.8 select_dynamic-update-slice_fusion.4
  313.6 6.7 %multiply_reduce_fusion.4 = f32[]{:T(128)} fusion(f32[1024,2048]{1,0:T(8,128)} %get-tuple-element.374, bf16[2048,768]{1,0:T(8,128)(2,1)} %get-tuple-element.373, s32[]{:T(128)S(6)} %select_n.40, bf16[1024,768]{0,1:T(8,128)(2,1)} %get-tuple-element.372), kind=kOutput, calls=%fused_computation.clone.1 | convolution fusion | flops 274726912 | bytes 9044996 | tf_op jit(solution)/shard_map/while/body/eval_jaxpr/dot_general | solution.py:28
  320.3 0.8 select_dynamic-update-slice_fusion.4
  321.1 6.7 %multiply_reduce_fusion.4 = f32[]{:T(128)} fusion(f32[1024,2048]{1,0:T(8,128)} %get-tuple-element.374, bf16[2048,768]{1,0:T(8,128)(2,1)} %get-tuple-element.373, s32[]{:T(128)S(6)} %select_n.40, bf16[1024,768]{0,1:T(8,128)(2,1)} %get-tuple-element.372), kind=kOutput, calls=%fused_computation.clone.1 | convolution fusion | flops 274726912 | bytes 9044996 | tf_op jit(solution)/shard_map/while/body/eval_jaxpr/dot_general | solution.py:28
  327.8 0.8 select_dynamic-update-slice_fusion.4
  328.6 6.7 %multiply_reduce_fusion.4 = f32[]{:T(128)} fusion(f32[1024,2048]{1,0:T(8,128)} %get-tuple-element.374, bf16[2048,768]{1,0:T(8,128)(2,1)} %get-tuple-element.373, s32[]{:T(128)S(6)} %select_n.40, bf16[1024,768]{0,1:T(8,128)(2,1)} %get-tuple-element.372), kind=kOutput, calls=%fused_computation.clone.1 | convolution fusion | flops 274726912 | bytes 9044996 | tf_op jit(solution)/shard_map/while/body/eval_jaxpr/dot_general | solution.py:28
  335.3 0.8 select_dynamic-update-slice_fusion.4
  336.1 6.7 %multiply_reduce_fusion.4 = f32[]{:T(128)} fusion(f32[1024,2048]{1,0:T(8,128)} %get-tuple-element.374, bf16[2048,768]{1,0:T(8,128)(2,1)} %get-tuple-element.373, s32[]{:T(128)S(6)} %select_n.40, bf16[1024,768]{0,1:T(8,128)(2,1)} %get-tuple-element.372), kind=kOutput, calls=%fused_computation.clone.1 | convolution fusion | flops 274726912 | bytes 9044996 | tf_op jit(solution)/shard_map/while/body/eval_jaxpr/dot_general | solution.py:28
  342.8 0.8 select_dynamic-update-slice_fusion.4
  343.6 39.3 %psum.7 = f32[12]{0:T(128)S(1)} all-reduce(f32[12]{0:T(128)S(1)} %add.106), channel_id=1, replica_groups=mesh['dp'=4,'fsdp'=8] {'dp','fsdp'}, use_global_device_ids=true, to_apply=%region_7.8 | all-reduce | flops 12 | bytes 96 | tf_op jit(solution)/shard_map/psum | solution.py:100
  383.3 26.4 %fusion.19 = (bf16[1792,2048]{1,0:T(8,128)(2,1)}, bf16[1792,2048]{1,0:T(8,128)(2,1)}, bf16[1792,2048]{1,0:T(8,128)(2,1)}) fusion(bf16[1792,2048]{1,0:T(8,128)(2,1)} %param.31, bf16[1792,2048]{1,0:T(8,128)(2,1)} %param.30, bf16[1792,2048]{1,0:T(8,128)(2,1)} %param.29, bf16[2048,768]{1,0:T(8,128)(2,1)} %get-tuple-element.418, ...), kind=kOutput, calls=%fused_computation.33 | convolution fusion | flops 5722013696 | bytes 49941504 | tf_op jit(solution)/shard_map/dot_general | solution.py:46
  409.7 16.0 %fusion.21 = (bf16[1024,2048]{1,0:T(8,128)(2,1)}, bf16[1024,2048]{1,0:T(8,128)(2,1)}, bf16[1024,2048]{1,0:T(8,128)(2,1)}) fusion(bf16[1024,2048]{1,0:T(8,128)(2,1)S(1)} %copy-done.1, bf16[1024,2048]{1,0:T(8,128)(2,1)S(1)} %copy-done.5, bf16[1024,2048]{1,0:T(8,128)(2,1)} %param.26, bf16[2048,768]{1,0:T(8,128)(2,1)S(1)} %copy-done.3, ...), kind=kOutput, calls=%fused_computation.36 | convolution fusion | flops 3269722112 | bytes 29887488 | tf_op jit(solution)/shard_map/dot_general | solution.py:46
  (28 shorter events, 1.2 us)
Async XLA Ops:
  7.2 24.8 %all-gather.5.cloned.1.call-start = ((), (), s32[]{:S(2)}) async-start(), calls=%async_computation | async-start | bytes 1966080 | tf_op jit(solution)/shard_map/all_gather | solution.py:83
  7.9 51.9 %all-gather.9.cloned.1.call-start = ((), (), s32[]{:S(2)}) async-start(), calls=%async_computation.2 | async-start | bytes 3440640 | tf_op jit(solution)/shard_map/all_gather | solution.py:84
  8.6 113.9 %all-gather.11.cloned.1.call-start = ((), (), s32[]{:S(2)}) async-start(), calls=%async_computation.3 | async-start | bytes 3538944 | tf_op jit(solution)/shard_map/all_gather | solution.py:94
  9.4 244.1 %all-gather.7.cloned.1.call-start = ((), (), s32[]{:S(2)}) async-start(), calls=%async_computation.1 | async-start | bytes 3538944 | tf_op jit(solution)/shard_map/all_gather | solution.py:93
  10.8 13.4 %copy-start = (bf16[1024,2048]{1,0:T(8,128)(2,1)S(1)}, bf16[1024,2048]{1,0:T(8,128)(2,1)}, u32[]{:S(2)}) copy-start(bf16[1024,2048]{1,0:T(8,128)(2,1)} %param.28) | copy-start | bytes 12582916
  253.5 129.5 %copy-start.4 = (s32[12]{0:T(128)S(1)}, s32[12]{0:T(128)}, u32[]{:S(2)}) copy-start(s32[12]{0:T(128)} %param.25) | copy-start | bytes 148
  383.3 26.4 %copy-start.1 = (bf16[1024,2048]{1,0:T(8,128)(2,1)S(1)}, bf16[1024,2048]{1,0:T(8,128)(2,1)}, u32[]{:S(2)}) copy-start(bf16[1024,2048]{1,0:T(8,128)(2,1)} %param.28) | copy-start | bytes 12582916
  383.3 26.4 %copy-start.2 = (bf16[1024,768]{0,1:T(8,128)(2,1)S(1)}, bf16[1024,768]{0,1:T(8,128)(2,1)}, u32[]{:S(2)}) copy-start(bf16[1024,768]{0,1:T(8,128)(2,1)} %get-tuple-element.415) | copy-start | bytes 4718596
  383.3 26.4 %copy-start.3 = (bf16[2048,768]{1,0:T(8,128)(2,1)S(1)}, bf16[2048,768]{1,0:T(8,128)(2,1)}, u32[]{:S(2)}) copy-start(bf16[2048,768]{1,0:T(8,128)(2,1)} %get-tuple-element.420) | copy-start | bytes 9437188
  383.3 26.4 %copy-start.5 = (bf16[1024,2048]{1,0:T(8,128)(2,1)S(1)}, bf16[1024,2048]{1,0:T(8,128)(2,1)}, u32[]{:S(2)}) copy-start(bf16[1024,2048]{1,0:T(8,128)(2,1)} %param.27) | copy-start | bytes 12582916
Sparse Core Ops, SparseCore 0:
  9.6 22.3 all-gather.4
  33.5 26.2 all-gather.8
  62.0 60.4 all-gather.10
  124.6 59.0 all-gather.6
where the time goes:
time: 433 us; the launch traced here: 432 us
  matrix products  244 us (56%)
  waiting for transfers between devices  90.2 us (21%)
  other arithmetic  44.6 us (10%)
  blocking collectives  39.3 us (9%)
  between operations  13.8 us (3%)
    dot_general x24, matrix products, one_example(): lax.dot_general(inputs_slot, grads_slot, (((1,), (1,)), ((), ())), prefer...  202 us
    all_gather x1, waiting for transfers between devices, per_device(): lax.all_gather(feedforward_cotangent, 'fsdp', axis=0, tiled=True)  60.6 us
    dot_general x2, matrix products, weighted_gradient(): lax.dot_general(scaled, cotangents, (((1,), (1,)), ((), ())), preferred_e...  42.3 us
    psum x1, blocking collectives, per_device(): norm_vals = lax.psum(attention_part + feedforward_part, ('dp', 'fsdp'))  39.3 us
    all_gather x1, waiting for transfers between devices, per_device(): lax.all_gather(feedforward_input, 'dp', axis=1, tiled=True)  25.2 us
    scatter x24, other arithmetic, one_example(): return norm_vals.at[example].set(jnp.sum(tile_block * tile_block * precond))  19.5 us
    div x2, other arithmetic, example_norms(): precond = 1.0 / (jnp.sqrt(second.astype(jnp.float32)) + epsilon)  19.4 us
  transfers between devices with their start and end apart: 4, of which 3 were waited for; matrix products, arithmetic and copies ran while one was open for 36% of the time, Pallas kernels for 0%

commit v1 on v0

--- a/solution.py
+++ b/solution.py
@@ -1,6 +1,10 @@
+import functools
+
 import jax
 import jax.numpy as jnp
 from jax import lax
+from jax.experimental import pallas as pl
+from jax.experimental.pallas import tpu as pltpu
 from jax.sharding import PartitionSpec as P
 
 first_decay = 0.9
@@ -120,9 +124,407 @@
     )
 
 
+MESH = pl.DeviceIdType.MESH
+TILE = 256
+GROUP = 256
+ROWS_PAD = 16
+VMEM_BYTES = 56 * 2**20
+
+
+def refined_reciprocal(value):
+    guess = pl.reciprocal(value, approx=True)
+    return guess * (2.0 - value * guess)
+
+
+def gather_kernel(
+    n, m, slot_len, example_count,
+    xa_in, xf_in, ca_in, cf_in, va_in, vf_in, live_ref, same_ref,
+    xa_out, xf_out, c_out,
+    xa_t, xf_t, x_rows, cbuf, vbuf, acc, norm_f, norm_d,
+    local_sem, out_sem, c_send, c_recv, x_send, x_recv, core_send, core_recv,
+    f_send, f_recv, d_send, d_recv,
+):
+    me_d, me_f = lax.axis_index("dp"), lax.axis_index("fsdp")
+    position = lax.select(lax.rem(me_f, 2) == 0, me_f // 2, n - 1 - me_f // 2)
+
+    def ring_index(place):
+        place = lax.rem(place + n, n)
+        return lax.select(place < n // 2, 2 * place, 2 * (n - 1 - place) + 1)
+
+    rows_a, rows_f = xa_in.shape[1], xf_in.shape[1]
+    share, block = xa_in.shape[0], ca_in.shape[0]
+    tiles_a, tiles_f = rows_a // TILE, rows_f // TILE
+    groups = live_ref.shape[1] // GROUP
+    per_group = GROUP // slot_len
+    high, core, m_high = me_d // 2, lax.rem(me_d, 2), m // 2
+
+    x_bufs = (xa_t, xf_t)
+
+    def x_slot(layer, owner):
+        return x_bufs[layer].at[pl.ds(pl.multiple_of(owner * share, 16), share)]
+
+    own = []
+    for index, (src, dst) in enumerate((
+        (ca_in, cbuf.at[0, me_f]),
+        (cf_in, cbuf.at[1, me_f]),
+        (xa_in, x_slot(0, me_d)),
+        (xf_in, x_slot(1, me_d)),
+        (va_in, vbuf.at[pl.ds(0, rows_a)]),
+        (vf_in, vbuf.at[pl.ds(rows_a, rows_f)]),
+    )):
+        copy = pltpu.make_async_copy(src, dst, local_sem.at[index])
+        copy.start()
+        own.append(copy)
+
+    barrier = pltpu.get_barrier_semaphore()
+    for k in range(1, n):
+        pl.semaphore_signal(
+            barrier, inc=1, device_id={"fsdp": lax.rem(me_f + k, n)}, device_id_type=MESH
+        )
+    for k in range(1, m):
+        pl.semaphore_signal(
+            barrier, inc=1, device_id={"dp": lax.rem(me_d + k, m)}, device_id_type=MESH
+        )
+    pl.semaphore_wait(barrier, n + m - 2)
+
+    def c_copy(layer, way, step):
+        sign = 1 - 2 * way
+        slot = cbuf.at[layer, ring_index(position - sign * step)]
+        return pltpu.make_async_remote_copy(
+            src_ref=slot, dst_ref=slot,
+            send_sem=c_send.at[layer, way, step], recv_sem=c_recv.at[layer, way, step],
+            device_id={"fsdp": ring_index(position + sign)}, device_id_type=MESH,
+        )
+
+    def x_copy(layer, k):
+        slot = x_slot(layer, me_d)
+        return pltpu.make_async_remote_copy(
+            src_ref=slot, dst_ref=slot,
+            send_sem=x_send.at[layer, k], recv_sem=x_recv.at[layer, k],
+            device_id={"dp": lax.rem(high + k, m_high) * 2 + core}, device_id_type=MESH,
+        )
+
+    def core_copy(layer, k):
+        slot = x_slot(layer, lax.rem(high + m_high - k, m_high) * 2 + core)
+        return pltpu.make_async_remote_copy(
+            src_ref=slot, dst_ref=slot,
+            send_sem=core_send.at[layer, k], recv_sem=core_recv.at[layer, k],
+            device_id={"dp": high * 2 + 1 - core}, device_id_type=MESH,
+        )
+
+    pairs = [(layer, way) for layer in range(2) for way in range(2)]
+    last = n // 2 - 1
+
+    def c_pairs(step):
+        return pairs if step < last else [(0, 0), (1, 1)]
+
+    for layer in range(2):
+        own[layer].wait()
+        for way in range(2):
+            c_copy(layer, way, 0).start()
+    for layer in range(2):
+        own[2 + layer].wait()
+        for k in range(1, m_high):
+            x_copy(layer, k).start()
+        core_copy(layer, 0).start()
+    acc[...] = jnp.zeros_like(acc)
+
+    def advance(step):
+        for layer, way in c_pairs(step):
+            c_copy(layer, way, step).wait_recv()
+            if (layer, way) in (c_pairs(step + 1) if step < last else []):
+                c_copy(layer, way, step + 1).start()
+
+    def take_inputs(layer):
+        for k in range(1, m_high):
+            x_copy(layer, k).wait_recv()
+            core_copy(layer, k).start()
+        for k in range(m_high):
+            core_copy(layer, k).wait_recv()
+        buf, base, tiles = x_bufs[layer], (0, rows_a)[layer], (tiles_a, tiles_f)[layer]
+
+        def turn(tile, carry):
+            here = pl.multiple_of(tile * TILE, TILE)
+            there = pl.multiple_of(base + tile * TILE, TILE)
+            for g in range(groups):
+                x_rows[g, pl.ds(there, TILE), :] = buf[
+                    pl.ds(g * GROUP, GROUP), pl.ds(here, TILE)
+                ].T
+            return carry
+
+        lax.fori_loop(0, tiles, turn, 0)
+
+    def unit(tile_from, tile_to, owner):
+        column = pl.multiple_of(owner * block, 128)
+
+        def one_tile(tile, carry):
+            layer = lax.select(tile < tiles_a, 0, 1)
+            row = pl.multiple_of(tile * TILE, TILE)
+            second = vbuf[pl.ds(row, TILE), pl.ds(column, block)].astype(jnp.float32)
+            precond = refined_reciprocal(second * lax.rsqrt(second) + epsilon)
+            for g in range(groups):
+                lhs = x_rows[g, pl.ds(row, TILE), :]
+                rhs = cbuf[layer, owner, :, pl.ds(g * GROUP, GROUP)]
+                for e in range(g * per_group, (g + 1) * per_group):
+                    live = live_ref[pl.ds(e, 1), pl.ds(g * GROUP, GROUP)].astype(jnp.bfloat16)
+                    product = lax.dot_general(
+                        lhs, rhs * live, (((1,), (1,)), ((), ())),
+                        preferred_element_type=jnp.float32,
+                    )
+                    square = product * product * precond
+                    acc[e] += jnp.sum(square.reshape(TILE // 8, 8, block), axis=0)
+            return carry
+
+        lax.fori_loop(tile_from, tile_to, one_tile, 0)
+
+    total_tiles = tiles_a + tiles_f
+
+    def both_ways(tile_from, tile_to, step):
+        def one_way(way, carry):
+            unit(tile_from, tile_to, ring_index(position - (1 - 2 * way) * (step + 1)))
+            return carry
+
+        lax.fori_loop(0, 2, one_way, 0)
+
+    own[4].wait()
+    own[5].wait()
+    take_inputs(0)
+    unit(0, tiles_a, me_f)
+    advance(0)
+    both_ways(0, tiles_a, 0)
+    take_inputs(1)
+    unit(tiles_a, total_tiles, me_f)
+    if last >= 1:
+        advance(1)
+        if last >= 2:
+            both_ways(tiles_a, total_tiles, 0)
+    for step in range(2, last + 1):
+        advance(step)
+        both_ways(0, total_tiles, step - 1)
+    unit(0, total_tiles, ring_index(position + n // 2))
+
+    c_store = pltpu.make_async_copy(cbuf, c_out, out_sem)
+    c_store.start()
+
+    partial = jnp.sum(jnp.sum(acc[...], axis=1), axis=1, keepdims=True)
+    norm_f[me_f] = jnp.broadcast_to(partial, (ROWS_PAD, 128))
+
+    def sum_over(axis, count, me, buf, send, recv):
+        copies = []
+        for k in range(1, count):
+            copy = pltpu.make_async_remote_copy(
+                src_ref=buf.at[me], dst_ref=buf.at[me],
+                send_sem=send.at[k], recv_sem=recv.at[k],
+                device_id={axis: lax.rem(me + k, count)}, device_id_type=MESH,
+            )
+            copy.start()
+            copies.append(copy)
+        for copy in copies:
+            copy.wait_recv()
+        return copies, jnp.sum(buf[...], axis=0)
+
+    f_copies, over_f = sum_over("fsdp", n, me_f, norm_f, f_send, f_recv)
+    norm_d[me_d] = over_f
+    d_copies, norm_vals = sum_over("dp", m, me_d, norm_d, d_send, d_recv)
+
+    strength = jnp.sqrt(norm_vals + norm_epsilon)
+    same = same_ref[...]
+    sub = lax.broadcasted_iota(jnp.int32, (ROWS_PAD, 128), 0)
+    lane = lax.broadcasted_iota(jnp.int32, (ROWS_PAD, 128), 1)
+    strength_row = jnp.sum(jnp.where(sub == lane, strength, 0.0), axis=0, keepdims=True)
+    group_total = jnp.sum(same * strength_row, axis=1, keepdims=True)
+    group_count = jnp.sum(same, axis=1, keepdims=True)
+    weights = group_count * strength[:, :1] / group_total
+    token_weight = jnp.sum(live_ref[...] * weights, axis=0, keepdims=True)
+
+    for layer, out in ((0, xa_out), (1, xf_out)):
+        base, tiles = (0, rows_a)[layer], (tiles_a, tiles_f)[layer]
+
+        def scale(tile, carry, out=out, base=base):
+            here = pl.multiple_of(tile * TILE, TILE)
+            there = pl.multiple_of(base + tile * TILE, TILE)
+            for g in range(groups):
+                lanes = slice(g * GROUP, (g + 1) * GROUP)
+                wide = x_rows[g, pl.ds(there, TILE), :].astype(jnp.float32)
+                out[pl.ds(here, TILE), lanes] = (wide * token_weight[:, lanes]).astype(jnp.bfloat16)
+            return carry
+
+        lax.fori_loop(0, tiles, scale, 0)
+
+    for step in range(last + 1):
+        for layer, way in c_pairs(step):
+            c_copy(layer, way, step).wait_send()
+    for layer in range(2):
+        for k in range(1, m_high):
+            x_copy(layer, k).wait_send()
+        for k in range(m_high):
+            core_copy(layer, k).wait_send()
+    for copy in f_copies + d_copies:
+        copy.wait_send()
+    c_store.wait()
+
+
+def gather_and_weigh(n, m, xa, xf, ca, cf, va, vf, lengths, groups):
+    example_count = lengths.shape[0]
+    tokens = ca.shape[1]
+    slot_len = tokens // example_count
+    live = live_tokens(lengths, slot_len)
+    example_of = jnp.arange(tokens, dtype=jnp.int32) // slot_len
+    row = jnp.arange(ROWS_PAD, dtype=jnp.int32)
+    live_hot = ((row[:, None] == example_of[None, :]) & live[None, :]).astype(jnp.float32)
+    padded = jnp.concatenate([groups, -1 - jnp.arange(128 - example_count, dtype=jnp.int32)])
+    same = (padded[:ROWS_PAD, None] == padded[None, :]).astype(jnp.float32)
+    rows_a, rows_f, block = xa.shape[0], xf.shape[0], ca.shape[0]
+    columns = n * block
+    bf16, f32 = jnp.bfloat16, jnp.float32
+    hbm = pl.BlockSpec(memory_space=pl.ANY)
+    vmem = pl.BlockSpec(memory_space=pltpu.VMEM)
+    dma = pltpu.SemaphoreType.DMA
+    return pl.pallas_call(
+        functools.partial(gather_kernel, n, m, slot_len, example_count),
+        out_shape=(
+            jax.ShapeDtypeStruct((rows_a, tokens), bf16),
+            jax.ShapeDtypeStruct((rows_f, tokens), bf16),
+            jax.ShapeDtypeStruct((2, n, block, tokens), bf16),
+        ),
+        in_specs=[hbm] * 6 + [vmem] * 2,
+        out_specs=(vmem, vmem, hbm),
+        scratch_shapes=[
+            pltpu.VMEM((tokens, rows_a), bf16),
+            pltpu.VMEM((tokens, rows_f), bf16),
+            pltpu.VMEM((tokens // GROUP, rows_a + rows_f, GROUP), bf16),
+            pltpu.VMEM((2, n, block, tokens), bf16),
+            pltpu.VMEM((rows_a + rows_f, columns), bf16),
+            pltpu.VMEM((ROWS_PAD, 8, block), f32),
+            pltpu.VMEM((n, ROWS_PAD, 128), f32),
+            pltpu.VMEM((m, ROWS_PAD, 128), f32),
+            dma((6,)),
+            dma,
+            dma((2, 2, n // 2)),
+            dma((2, 2, n // 2)),
+            dma((2, m // 2)),
+            dma((2, m // 2)),
+            dma((2, m // 2)),
+            dma((2, m // 2)),
+            dma((n,)),
+            dma((n,)),
+            dma((m,)),
+            dma((m,)),
+        ],
+        compiler_params=pltpu.CompilerParams(
+            collective_id=0, has_side_effects=True, vmem_limit_bytes=VMEM_BYTES
+        ),
+        name="gather_and_weigh",
+    )(xa.T, xf.T, ca, cf, va, vf, live_hot, same)
+
+
+def update_kernel(example_count, x_ref, c_ref, w_ref, m_ref, v_ref, w_out, m_out, v_out):
+    scaled = x_ref[...]
+    for j in range(w_ref.shape[1] // TILE):
+        cols = slice(j * TILE, (j + 1) * TILE)
+        gradient = lax.dot_general(
+            scaled, c_ref[0, cols, :], (((1,), (1,)), ((), ())),
+            preferred_element_type=jnp.float32,
+        ) * (1.0 / example_count)
+        moment_new = first_decay * m_ref[:, cols].astype(jnp.float32) + (1.0 - first_decay) * gradient
+        second_new = (
+            second_decay * v_ref[:, cols].astype(jnp.float32)
+            + (1.0 - second_decay) * (gradient * gradient)
+        )
+        unbiased = second_new * (1.0 / second_bias)
+        root = unbiased * lax.rsqrt(unbiased)
+        step_dir = moment_new * (1.0 / first_bias) * refined_reciprocal(root + epsilon)
+        weight = w_ref[:, cols].astype(jnp.float32)
+        updated = (1.0 - learn_rate * weight_decay) * weight - learn_rate * step_dir
+        w_out[:, cols] = updated.astype(jnp.bfloat16)
+        m_out[:, cols] = moment_new.astype(jnp.bfloat16)
+        v_out[:, cols] = second_new.astype(jnp.bfloat16)
+
+
+def update(layer, example_count, scaled, cotangents, weight, moment, second):
+    rows, columns = weight.shape
+    tokens = scaled.shape[1]
+    state = pl.BlockSpec((TILE, columns), lambda i: (i, 0))
+    shape = jax.ShapeDtypeStruct((rows, columns), jnp.bfloat16)
+    return pl.pallas_call(
+        functools.partial(update_kernel, example_count),
+        grid=(rows // TILE,),
+        in_specs=[
+            pl.BlockSpec((TILE, tokens), lambda i: (i, 0)),
+            pl.BlockSpec((1, columns, tokens), lambda i: (layer, 0, 0)),
+            state,
+            state,
+            state,
+        ],
+        out_specs=(state, state, state),
+        out_shape=(shape, shape, shape),
+        compiler_params=pltpu.CompilerParams(vmem_limit_bytes=VMEM_BYTES),
+        name="update",
+    )(scaled, cotangents, weight, moment, second)
+
+
+def per_device_kernels(
+    n, m,
+    attention_input,
+    feedforward_input,
+    attention_cotangent,
+    feedforward_cotangent,
+    lengths,
+    groups,
+    attention_weight,
+    attention_moment,
+    attention_second,
+    feedforward_weight,
+    feedforward_moment,
+    feedforward_second,
+):
+    example_count = lengths.shape[0]
+    xa, xf, gathered = gather_and_weigh(
+        n, m, attention_input, feedforward_input, attention_cotangent, feedforward_cotangent,
+        attention_second, feedforward_second, lengths, groups,
+    )
+    gathered = gathered.reshape(2, -1, gathered.shape[3])
+    attention_new = update(
+        0, example_count, xa, gathered, attention_weight, attention_moment, attention_second
+    )
+    feedforward_new = update(
+        1, example_count, xf, gathered, feedforward_weight, feedforward_moment, feedforward_second
+    )
+    return attention_new + feedforward_new
+
+
+def fits_kernels(n, m, xa, xf, ca, lengths):
+    examples = lengths.shape[0]
+    tokens = ca.shape[1]
+    return (
+        n % 2 == 0
+        and n >= 6
+        and m % 2 == 0
+        and examples <= ROWS_PAD
+        and tokens % GROUP == 0
+        and GROUP % (tokens // examples) == 0
+        and ca.shape[0] // (n * m) == TILE
+        and xa.shape[0] // n % TILE == 0
+        and xf.shape[0] // n % TILE == 0
+        and tokens // m % 16 == 0
+    )
+
+
 def solution(mesh):
+    n, m = mesh.shape["fsdp"], mesh.shape["dp"]
+
+    def step(*arrays):
+        xa, xf, ca, _, lengths = arrays[:5]
+        if fits_kernels(n, m, xa, xf, ca, lengths):
+            return sharded(mesh, functools.partial(per_device_kernels, n, m))(*arrays)
+        return sharded(mesh, per_device)(*arrays)
+
+    return step
+
+
+def sharded(mesh, body):
     return jax.shard_map(
-        per_device,
+        body,
         mesh=mesh,
         in_specs=(
             P("fsdp", "dp"),

time: 433 us -> 149 us (0.34)
  matrix products: 244 us -> 0 us
  Pallas kernels: 0 us -> 145 us
  waiting for transfers between devices: 90.2 us -> 0 us
  other arithmetic: 44.6 us -> 2.77 us
  blocking collectives: 39.3 us -> 0 us
  between operations: 13.8 us -> 0.65 us
    dot_general x26 -> x0, matrix products: 244 us -> none  [the longest x24 202 us: one_example(): lax.dot_general(inputs_slot, grads_slot, (((1,), (1,)), ((), ())), prefer...]
    pallas_call x0 -> x3, Pallas kernels: none -> 145 us  [the longest x1 106 us: gather_and_weigh(): pl.pallas_call(functools.partial(gather_kernel, n, m, slot_len, example_c...]
    all_gather x4 -> x0, waiting for transfers between devices: 87.6 us -> none  [the longest x1 60.6 us: per_device(): lax.all_gather(feedforward_cotangent, 'fsdp', axis=0, tiled=True)]
    psum x1 -> x0, blocking collectives: 39.3 us -> none  [per_device(): norm_vals = lax.psum(attention_part + feedforward_part, ('dp', 'fsdp'))]
    scatter x24 -> x0, other arithmetic: 19.5 us -> none  [one_example(): return norm_vals.at[example].set(jnp.sum(tile_block * tile_block * precond))]
    div x3 -> x0, other arithmetic: 19.4 us -> none  [the longest x2 19.4 us: example_norms(): precond = 1.0 / (jnp.sqrt(second.astype(jnp.float32)) + epsilon)]
    select_n x2 -> x1, other arithmetic: 4.76 us -> 0.01 us  [gather_and_weigh(): example_of = jnp.arange(tokens, dtype=jnp.int32) // slot_len]
  transfers between devices with their start and end apart: 4 -> 0, of which waited for: 3 -> 0; matrix products, arithmetic and copies ran while one was open for 36% -> 0% of each run, Pallas kernels for 0% -> 0%
where the time goes in v1:
time: 149 us
  Pallas kernels  145 us (97%)
  other arithmetic  2.77 us (2%)
    pallas_call x1, Pallas kernels, gather_and_weigh(): pl.pallas_call(functools.partial(gather_kernel, n, m, slot_len, example_c...  106 us
    pallas_call x2, Pallas kernels, update(): pl.pallas_call(functools.partial(update_kernel, example_count), grid=(row...  39.2 us

profile of v1, /device:TPU:0, one launch (start us, length us, event | category | flops | bytes accessed | tf_op | source)
XLA Modules:
  0.0 148.6 jit_solution(6003205697956214211)
XLA Ops:
  0.6 0.7 pad_add_fusion
  1.4 0.7 compare_convert_fusion.same_ref
  2.1 0.7 iota_compare_fusion.1
  2.8 0.1 lt.17
  2.9 0.6 fusion.1.live_ref
  3.5 105.9 %gather_and_weigh.1 = (bf16[1024,768]{1,0:T(8,128)(2,1)}, bf16[1792,768]{1,0:T(8,128)(2,1)}, bf16[2,8,256,768]{3,2,1,0:T(8,128)(2,1)}) custom-call(bf16[192,1024]{1,0:T(8,128)(2,1)} %bitcast.7, bf16[192,1792]{1,0:T(8,128)(2,1)} %bitcast.6, bf16[256,768]{1,0:T(8,128)(2,1)} %ca_in.1, bf16[256,768]{1,0:T(8,128)(2,1)} %cf_in.1, bf16[1024,2048]{1,0:T(8,128)(2,1)} %v_ref.2, ...), custom_call_target="tpu_custom_call" | custom-call | tf_op jit(solution)/shard_map/gather_and_weigh/pallas_call | solution.py:383
  109.4 23.8 %update.3 = (bf16[1792,2048]{1,0:T(8,128)(2,1)}, bf16[1792,2048]{1,0:T(8,128)(2,1)}, bf16[1792,2048]{1,0:T(8,128)(2,1)}) custom-call(bf16[1792,768]{1,0:T(8,128)(2,1)} %get-tuple-element.20.x_ref, bf16[2,2048,768]{2,1,0:T(8,128)(2,1)} %bitcast.4, bf16[1792,2048]{1,0:T(8,128)(2,1)} %w_ref.3, bf16[1792,2048]{1,0:T(8,128)(2,1)} %m_ref.3, bf16[1792,2048]{1,0:T(8,128)(2,1)} %v_ref.3), custom_call_target="tpu_custom_call" | custom-call | tf_op jit(solution)/shard_map/update/pallas_call | solution.py:449
  133.2 15.3 %update.2 = (bf16[1024,2048]{1,0:T(8,128)(2,1)}, bf16[1024,2048]{1,0:T(8,128)(2,1)}, bf16[1024,2048]{1,0:T(8,128)(2,1)}) custom-call(bf16[1024,768]{1,0:T(8,128)(2,1)} %get-tuple-element.15.x_ref, bf16[2,2048,768]{2,1,0:T(8,128)(2,1)} %bitcast.5, bf16[1024,2048]{1,0:T(8,128)(2,1)} %w_ref.2, bf16[1024,2048]{1,0:T(8,128)(2,1)} %m_ref.2, bf16[1024,2048]{1,0:T(8,128)(2,1)} %v_ref.2), custom_call_target="tpu_custom_call" | custom-call | tf_op jit(solution)/shard_map/update/pallas_call | solution.py:449
  (2 shorter events, 0.0 us)

commit v2 on v1

--- a/solution.py
+++ b/solution.py
@@ -126,21 +126,21 @@
 
 MESH = pl.DeviceIdType.MESH
 TILE = 256
-GROUP = 256
+GROUP = 128
 ROWS_PAD = 16
 VMEM_BYTES = 56 * 2**20
 
 
-def refined_reciprocal(value):
-    guess = pl.reciprocal(value, approx=True)
-    return guess * (2.0 - value * guess)
+def inverse_root(value):
+    guess = lax.rsqrt(value)
+    return guess * (2.0 - (value * guess + epsilon) * guess)
 
 
 def gather_kernel(
     n, m, slot_len, example_count,
     xa_in, xf_in, ca_in, cf_in, va_in, vf_in, live_ref, same_ref,
     xa_out, xf_out, c_out,
-    xa_t, xf_t, x_rows, cbuf, vbuf, acc, norm_f, norm_d,
+    xa_t, xf_t, x_rows, cbuf, ct, picked, vbuf, acc, norm_f, norm_d,
     local_sem, out_sem, c_send, c_recv, x_send, x_recv, core_send, core_recv,
     f_send, f_recv, d_send, d_recv,
 ):
@@ -228,6 +228,8 @@
             x_copy(layer, k).start()
         core_copy(layer, 0).start()
     acc[...] = jnp.zeros_like(acc)
+    picked[...] = jnp.zeros_like(picked)
+    alive = jnp.sum(live_ref[...], axis=0, keepdims=True).astype(jnp.bfloat16)
 
     def advance(step):
         for layer, way in c_pairs(step):
@@ -254,34 +256,36 @@
 
         lax.fori_loop(0, tiles, turn, 0)
 
-    def unit(tile_from, tile_to, owner):
+    def unit(layer, owner):
         column = pl.multiple_of(owner * block, 128)
+        tile_from, tile_to = ((0, tiles_a), (tiles_a, tiles_a + tiles_f))[layer]
+        for g in range(groups):
+            lanes = slice(g * GROUP, (g + 1) * GROUP)
+            turned = (cbuf[layer, owner, :, pl.ds(g * GROUP, GROUP)] * alive[:, lanes]).T
+            ct[layer, pl.ds(g * GROUP, GROUP), pl.ds(column, block)] = turned
+            for q in range(per_group):
+                rows = slice(q * slot_len, (q + 1) * slot_len)
+                picked[g * per_group + q, rows, :] = turned[rows]
 
         def one_tile(tile, carry):
-            layer = lax.select(tile < tiles_a, 0, 1)
             row = pl.multiple_of(tile * TILE, TILE)
             second = vbuf[pl.ds(row, TILE), pl.ds(column, block)].astype(jnp.float32)
-            precond = refined_reciprocal(second * lax.rsqrt(second) + epsilon)
-            for g in range(groups):
-                lhs = x_rows[g, pl.ds(row, TILE), :]
-                rhs = cbuf[layer, owner, :, pl.ds(g * GROUP, GROUP)]
-                for e in range(g * per_group, (g + 1) * per_group):
-                    live = live_ref[pl.ds(e, 1), pl.ds(g * GROUP, GROUP)].astype(jnp.bfloat16)
-                    product = lax.dot_general(
-                        lhs, rhs * live, (((1,), (1,)), ((), ())),
-                        preferred_element_type=jnp.float32,
-                    )
-                    square = product * product * precond
-                    acc[e] += jnp.sum(square.reshape(TILE // 8, 8, block), axis=0)
+            precond = inverse_root(second)
+            for e in range(example_count):
+                product = jnp.dot(
+                    x_rows[e // per_group, pl.ds(row, TILE), :], picked[e],
+                    preferred_element_type=jnp.float32,
+                )
+                square = product * product * precond
+                acc[e] += jnp.sum(square.reshape(TILE // 8, 8, block), axis=0)
             return carry
 
         lax.fori_loop(tile_from, tile_to, one_tile, 0)
 
-    total_tiles = tiles_a + tiles_f
-
-    def both_ways(tile_from, tile_to, step):
+    def both_ways(layers, step):
         def one_way(way, carry):
-            unit(tile_from, tile_to, ring_index(position - (1 - 2 * way) * (step + 1)))
+            for layer in layers:
+                unit(layer, ring_index(position - (1 - 2 * way) * (step + 1)))
             return carry
 
         lax.fori_loop(0, 2, one_way, 0)
@@ -289,21 +293,20 @@
     own[4].wait()
     own[5].wait()
     take_inputs(0)
-    unit(0, tiles_a, me_f)
+    unit(0, me_f)
     advance(0)
-    both_ways(0, tiles_a, 0)
+    both_ways((0,), 0)
     take_inputs(1)
-    unit(tiles_a, total_tiles, me_f)
-    if last >= 1:
-        advance(1)
-        if last >= 2:
-            both_ways(tiles_a, total_tiles, 0)
+    unit(1, me_f)
+    advance(1)
+    both_ways((1,), 0)
     for step in range(2, last + 1):
         advance(step)
-        both_ways(0, total_tiles, step - 1)
-    unit(0, total_tiles, ring_index(position + n // 2))
-
-    c_store = pltpu.make_async_copy(cbuf, c_out, out_sem)
+        both_ways((0, 1), step - 1)
+    for layer in range(2):
+        unit(layer, ring_index(position + n // 2))
+
+    c_store = pltpu.make_async_copy(ct, c_out, out_sem)
     c_store.start()
 
     partial = jnp.sum(jnp.sum(acc[...], axis=1), axis=1, keepdims=True)
@@ -385,7 +388,7 @@
         out_shape=(
             jax.ShapeDtypeStruct((rows_a, tokens), bf16),
             jax.ShapeDtypeStruct((rows_f, tokens), bf16),
-            jax.ShapeDtypeStruct((2, n, block, tokens), bf16),
+            jax.ShapeDtypeStruct((2, tokens, columns), bf16),
         ),
         in_specs=[hbm] * 6 + [vmem] * 2,
         out_specs=(vmem, vmem, hbm),
@@ -394,6 +397,8 @@
             pltpu.VMEM((tokens, rows_f), bf16),
             pltpu.VMEM((tokens // GROUP, rows_a + rows_f, GROUP), bf16),
             pltpu.VMEM((2, n, block, tokens), bf16),
+            pltpu.VMEM((2, tokens, columns), bf16),
+            pltpu.VMEM((example_count, GROUP, block), bf16),
             pltpu.VMEM((rows_a + rows_f, columns), bf16),
             pltpu.VMEM((ROWS_PAD, 8, block), f32),
             pltpu.VMEM((n, ROWS_PAD, 128), f32),
@@ -422,20 +427,18 @@
     scaled = x_ref[...]
     for j in range(w_ref.shape[1] // TILE):
         cols = slice(j * TILE, (j + 1) * TILE)
-        gradient = lax.dot_general(
-            scaled, c_ref[0, cols, :], (((1,), (1,)), ((), ())),
-            preferred_element_type=jnp.float32,
-        ) * (1.0 / example_count)
-        moment_new = first_decay * m_ref[:, cols].astype(jnp.float32) + (1.0 - first_decay) * gradient
-        second_new = (
-            second_decay * v_ref[:, cols].astype(jnp.float32)
-            + (1.0 - second_decay) * (gradient * gradient)
-        )
-        unbiased = second_new * (1.0 / second_bias)
-        root = unbiased * lax.rsqrt(unbiased)
-        step_dir = moment_new * (1.0 / first_bias) * refined_reciprocal(root + epsilon)
+        product = jnp.dot(scaled, c_ref[0, :, cols], preferred_element_type=jnp.float32)
+        moment_new = first_decay * m_ref[:, cols].astype(jnp.float32) + (
+            (1.0 - first_decay) / example_count
+        ) * product
+        second_new = second_decay * v_ref[:, cols].astype(jnp.float32) + (
+            (1.0 - second_decay) / example_count**2
+        ) * (product * product)
+        inverse = inverse_root(second_new * (1.0 / second_bias))
         weight = w_ref[:, cols].astype(jnp.float32)
-        updated = (1.0 - learn_rate * weight_decay) * weight - learn_rate * step_dir
+        updated = (1.0 - learn_rate * weight_decay) * weight - (
+            (learn_rate / first_bias) * moment_new
+        ) * inverse
         w_out[:, cols] = updated.astype(jnp.bfloat16)
         m_out[:, cols] = moment_new.astype(jnp.bfloat16)
         v_out[:, cols] = second_new.astype(jnp.bfloat16)
@@ -451,7 +454,7 @@
         grid=(rows // TILE,),
         in_specs=[
             pl.BlockSpec((TILE, tokens), lambda i: (i, 0)),
-            pl.BlockSpec((1, columns, tokens), lambda i: (layer, 0, 0)),
+            pl.BlockSpec((1, tokens, columns), lambda i: (layer, 0, 0)),
             state,
             state,
             state,
@@ -483,7 +486,6 @@
         n, m, attention_input, feedforward_input, attention_cotangent, feedforward_cotangent,
         attention_second, feedforward_second, lengths, groups,
     )
-    gathered = gathered.reshape(2, -1, gathered.shape[3])
     attention_new = update(
         0, example_count, xa, gathered, attention_weight, attention_moment, attention_second
     )
@@ -503,6 +505,7 @@
         and examples <= ROWS_PAD
         and tokens % GROUP == 0
         and GROUP % (tokens // examples) == 0
+        and (tokens // examples) % 16 == 0
         and ca.shape[0] // (n * m) == TILE
         and xa.shape[0] // n % TILE == 0
         and xf.shape[0] // n % TILE == 0

time: 149 us -> 145 us (0.973)
  Pallas kernels: 145 us -> 141 us
    pallas_call x1, Pallas kernels: 106 us -> 103 us  [gather_and_weigh(): pl.pallas_call(functools.partial(gather_kernel, n, m, slot_len, example_c...]
where the time goes in v2:
time: 145 us
  Pallas kernels  141 us (97%)
  other arithmetic  2.77 us (2%)
    pallas_call x1, Pallas kernels, gather_and_weigh(): pl.pallas_call(functools.partial(gather_kernel, n, m, slot_len, example_c...  103 us
    pallas_call x2, Pallas kernels, update(): pl.pallas_call(functools.partial(update_kernel, example_count), grid=(row...  38.6 us

profile of v2, /device:TPU:0, one launch (start us, length us, event | category | flops | bytes accessed | tf_op | source)
XLA Modules:
  0.0 144.6 jit_solution(5034089907541331410)
XLA Ops:
  0.6 0.7 pad_add_fusion
  1.4 0.7 compare_convert_fusion.same_ref
  2.1 0.7 iota_compare_fusion.1
  2.8 0.1 lt.17
  2.9 0.6 fusion.1.live_ref
  3.5 102.5 %gather_and_weigh.1 = (bf16[1024,768]{1,0:T(8,128)(2,1)}, bf16[1792,768]{1,0:T(8,128)(2,1)}, bf16[2,768,2048]{2,1,0:T(8,128)(2,1)}) custom-call(bf16[192,1024]{1,0:T(8,128)(2,1)} %bitcast.4, bf16[192,1792]{1,0:T(8,128)(2,1)} %bitcast.3, bf16[256,768]{1,0:T(8,128)(2,1)} %ca_in.1, bf16[256,768]{1,0:T(8,128)(2,1)} %cf_in.1, bf16[1024,2048]{1,0:T(8,128)(2,1)} %v_ref.2, ...), custom_call_target="tpu_custom_call" | custom-call | tf_op jit(solution)/shard_map/gather_and_weigh/pallas_call | solution.py:386
  106.0 23.5 %update.3 = (bf16[1792,2048]{1,0:T(8,128)(2,1)}, bf16[1792,2048]{1,0:T(8,128)(2,1)}, bf16[1792,2048]{1,0:T(8,128)(2,1)}) custom-call(bf16[1792,768]{1,0:T(8,128)(2,1)} %get-tuple-element.20.x_ref, bf16[2,768,2048]{2,1,0:T(8,128)(2,1)} %get-tuple-element.16.c_ref, bf16[1792,2048]{1,0:T(8,128)(2,1)} %w_ref.3, bf16[1792,2048]{1,0:T(8,128)(2,1)} %m_ref.3, ...), custom_call_target="tpu_custom_call" | custom-call | tf_op jit(solution)/shard_map/update/pallas_call | solution.py:452
  129.6 15.1 %update.2 = (bf16[1024,2048]{1,0:T(8,128)(2,1)}, bf16[1024,2048]{1,0:T(8,128)(2,1)}, bf16[1024,2048]{1,0:T(8,128)(2,1)}) custom-call(bf16[1024,768]{1,0:T(8,128)(2,1)} %get-tuple-element.15.x_ref, bf16[2,768,2048]{2,1,0:T(8,128)(2,1)} %get-tuple-element.16.c_ref, bf16[1024,2048]{1,0:T(8,128)(2,1)} %w_ref.2, bf16[1024,2048]{1,0:T(8,128)(2,1)} %m_ref.2, ...), custom_call_target="tpu_custom_call" | custom-call | tf_op jit(solution)/shard_map/update/pallas_call | solution.py:452
  (2 shorter events, 0.0 us)

commit v3 on v2

--- a/solution.py
+++ b/solution.py
@@ -138,9 +138,9 @@
 
 def gather_kernel(
     n, m, slot_len, example_count,
-    xa_in, xf_in, ca_in, cf_in, va_in, vf_in, live_ref, same_ref,
+    xa_in, xf_in, ca_in, cf_in, va_in, vf_in, lengths_ref, groups_ref,
     xa_out, xf_out, c_out,
-    xa_t, xf_t, x_rows, cbuf, ct, picked, vbuf, acc, norm_f, norm_d,
+    xa_t, xf_t, x_rows, cbuf, ct, picked, live_ref, vbuf, acc, norm_f, norm_d,
     local_sem, out_sem, c_send, c_recv, x_send, x_recv, core_send, core_recv,
     f_send, f_recv, d_send, d_recv,
 ):
@@ -229,6 +229,15 @@
         core_copy(layer, 0).start()
     acc[...] = jnp.zeros_like(acc)
     picked[...] = jnp.zeros_like(picked)
+    token = lax.broadcasted_iota(jnp.int32, (ROWS_PAD, live_ref.shape[1]), 1)
+    token_row = lax.broadcasted_iota(jnp.int32, (ROWS_PAD, live_ref.shape[1]), 0)
+    offset = token - token_row * slot_len
+    limit = jnp.zeros_like(token)
+    for e in range(example_count):
+        limit = jnp.where(token_row == e, lengths_ref[e], limit)
+    live_ref[...] = jnp.where(
+        (offset >= 0) & (offset < jnp.minimum(limit, slot_len)), 1.0, 0.0
+    ).astype(jnp.float32)
     alive = jnp.sum(live_ref[...], axis=0, keepdims=True).astype(jnp.bfloat16)
 
     def advance(step):
@@ -290,6 +299,10 @@
 
         lax.fori_loop(0, 2, one_way, 0)
 
+    def one_side(way, step):
+        for layer in range(2):
+            unit(layer, ring_index(position - (1 - 2 * way) * (step + 1)))
+
     own[4].wait()
     own[5].wait()
     take_inputs(0)
@@ -301,8 +314,9 @@
     advance(1)
     both_ways((1,), 0)
     for step in range(2, last + 1):
+        one_side(0, step - 1)
         advance(step)
-        both_ways((0, 1), step - 1)
+        one_side(1, step - 1)
     for layer in range(2):
         unit(layer, ring_index(position + n // 2))
 
@@ -331,9 +345,13 @@
     d_copies, norm_vals = sum_over("dp", m, me_d, norm_d, d_send, d_recv)
 
     strength = jnp.sqrt(norm_vals + norm_epsilon)
-    same = same_ref[...]
     sub = lax.broadcasted_iota(jnp.int32, (ROWS_PAD, 128), 0)
     lane = lax.broadcasted_iota(jnp.int32, (ROWS_PAD, 128), 1)
+    row_group, lane_group = -1 - sub, -1 - lane
+    for e in range(example_count):
+        row_group = jnp.where(sub == e, groups_ref[e], row_group)
+        lane_group = jnp.where(lane == e, groups_ref[e], lane_group)
+    same = jnp.where(row_group == lane_group, 1.0, 0.0).astype(jnp.float32)
     strength_row = jnp.sum(jnp.where(sub == lane, strength, 0.0), axis=0, keepdims=True)
     group_total = jnp.sum(same * strength_row, axis=1, keepdims=True)
     group_count = jnp.sum(same, axis=1, keepdims=True)
@@ -371,12 +389,6 @@
     example_count = lengths.shape[0]
     tokens = ca.shape[1]
     slot_len = tokens // example_count
-    live = live_tokens(lengths, slot_len)
-    example_of = jnp.arange(tokens, dtype=jnp.int32) // slot_len
-    row = jnp.arange(ROWS_PAD, dtype=jnp.int32)
-    live_hot = ((row[:, None] == example_of[None, :]) & live[None, :]).astype(jnp.float32)
-    padded = jnp.concatenate([groups, -1 - jnp.arange(128 - example_count, dtype=jnp.int32)])
-    same = (padded[:ROWS_PAD, None] == padded[None, :]).astype(jnp.float32)
     rows_a, rows_f, block = xa.shape[0], xf.shape[0], ca.shape[0]
     columns = n * block
     bf16, f32 = jnp.bfloat16, jnp.float32
@@ -390,7 +402,7 @@
             jax.ShapeDtypeStruct((rows_f, tokens), bf16),
             jax.ShapeDtypeStruct((2, tokens, columns), bf16),
         ),
-        in_specs=[hbm] * 6 + [vmem] * 2,
+        in_specs=[hbm] * 6 + [pl.BlockSpec(memory_space=pltpu.SMEM)] * 2,
         out_specs=(vmem, vmem, hbm),
         scratch_shapes=[
             pltpu.VMEM((tokens, rows_a), bf16),
@@ -399,6 +411,7 @@
             pltpu.VMEM((2, n, block, tokens), bf16),
             pltpu.VMEM((2, tokens, columns), bf16),
             pltpu.VMEM((example_count, GROUP, block), bf16),
+            pltpu.VMEM((ROWS_PAD, tokens), f32),
             pltpu.VMEM((rows_a + rows_f, columns), bf16),
             pltpu.VMEM((ROWS_PAD, 8, block), f32),
             pltpu.VMEM((n, ROWS_PAD, 128), f32),
@@ -420,7 +433,7 @@
             collective_id=0, has_side_effects=True, vmem_limit_bytes=VMEM_BYTES
         ),
         name="gather_and_weigh",
-    )(xa.T, xf.T, ca, cf, va, vf, live_hot, same)
+    )(xa.T, xf.T, ca, cf, va, vf, lengths, groups)
 
 
 def update_kernel(example_count, x_ref, c_ref, w_ref, m_ref, v_ref, w_out, m_out, v_out):

time: 145 us -> 135 us (0.931)
  Pallas kernels: 141 us -> 134 us
  other arithmetic: 2.77 us -> 0 us
    pallas_call x1, Pallas kernels: 103 us -> 95.6 us  [gather_and_weigh(): pl.pallas_call(functools.partial(gather_kernel, n, m, slot_len, example_c...]
where the time goes in v3:
time: 135 us
  Pallas kernels  134 us (99%)
    pallas_call x1, Pallas kernels, gather_and_weigh(): pl.pallas_call(functools.partial(gather_kernel, n, m, slot_len, example_c...  95.6 us
    pallas_call x2, Pallas kernels, update(): pl.pallas_call(functools.partial(update_kernel, example_count), grid=(row...  38.8 us

profile of v3, /device:TPU:0, one launch (start us, length us, event | category | flops | bytes accessed | tf_op | source)
XLA Modules:
  0.0 135.0 jit_solution(10445803169562138920)
XLA Ops:
  0.6 95.6 %gather_and_weigh.1 = (bf16[1024,768]{1,0:T(8,128)(2,1)}, bf16[1792,768]{1,0:T(8,128)(2,1)}, bf16[2,768,2048]{2,1,0:T(8,128)(2,1)}) custom-call(bf16[192,1024]{1,0:T(8,128)(2,1)} %bitcast.3, bf16[192,1792]{1,0:T(8,128)(2,1)} %bitcast.2, bf16[256,768]{1,0:T(8,128)(2,1)} %ca_in.1, bf16[256,768]{1,0:T(8,128)(2,1)} %cf_in.1, bf16[1024,2048]{1,0:T(8,128)(2,1)} %v_ref.2, ...), custom_call_target="tpu_custom_call" | custom-call | tf_op jit(solution)/shard_map/gather_and_weigh/pallas_call | solution.py:398
  96.3 23.7 %update.3 = (bf16[1792,2048]{1,0:T(8,128)(2,1)}, bf16[1792,2048]{1,0:T(8,128)(2,1)}, bf16[1792,2048]{1,0:T(8,128)(2,1)}) custom-call(bf16[1792,768]{1,0:T(8,128)(2,1)} %get-tuple-element.20.x_ref, bf16[2,768,2048]{2,1,0:T(8,128)(2,1)} %get-tuple-element.16.c_ref, bf16[1792,2048]{1,0:T(8,128)(2,1)} %w_ref.3, bf16[1792,2048]{1,0:T(8,128)(2,1)} %m_ref.3, ...), custom_call_target="tpu_custom_call" | custom-call | tf_op jit(solution)/shard_map/update/pallas_call | solution.py:465
  119.9 15.1 %update.2 = (bf16[1024,2048]{1,0:T(8,128)(2,1)}, bf16[1024,2048]{1,0:T(8,128)(2,1)}, bf16[1024,2048]{1,0:T(8,128)(2,1)}) custom-call(bf16[1024,768]{1,0:T(8,128)(2,1)} %get-tuple-element.15.x_ref, bf16[2,768,2048]{2,1,0:T(8,128)(2,1)} %get-tuple-element.16.c_ref, bf16[1024,2048]{1,0:T(8,128)(2,1)} %w_ref.2, bf16[1024,2048]{1,0:T(8,128)(2,1)} %m_ref.2, ...), custom_call_target="tpu_custom_call" | custom-call | tf_op jit(solution)/shard_map/update/pallas_call | solution.py:465
